TPU v7x, 256 devices: a whole 4x4x8 slice. The times are simulated.
256 devices in a mesh: tok: 64 (over y, z, core), head: 4 (over x).
Axes of the slice: x: 4, y: 4, z: 8, core: 2. Of those that a mesh axis runs over, the one named last changes fastest.
Arguments:
- queries: bfloat16 [2, 16384, 16, 256], P(None, 'tok', 'head'), may hold values from -6 to 6
- key_input: bfloat16 [2, 16384, 16, 256], P(None, 'tok', 'head'), may hold values from -6 to 6
- value_input: bfloat16 [2, 16384, 16, 256], P(None, 'tok', 'head'), may hold values from -6 to 6
- token_rates: float32 [2, 16, 16384], P(None, 'head', 'tok'), may hold values from 0.05 to 1
- fast_weights: float32 [16, 3, 256, 256], P('head'), may hold values from -0.375 to 0.375
- update_rate: float32 [16, 3], P('head'), may hold values from 0.2 to 1
- out_gain: float32 [16, 256], P('head'), may hold values from 0.5 to 1.5
Outputs:
- transformed: bfloat16 [2, 16384, 16, 256], P(None, 'tok', 'head')
All inputs are finite; a program needn't handle non-finite values.
Results may differ from a plain program's by a relative error of at most 0.029.
Values may be sent and summed in bfloat16 or wider, within the bound.
A program may use at most 64 MiB of HBM per device.

v0:
```python
import jax
import jax.numpy as jnp
from jax import lax
from jax.sharding import PartitionSpec as P

NS_STEPS = 3


coef_a = 3.4445
coef_b = -4.775
coef_c = 2.0315


def per_device(queries, key_input, value_input, token_rates, fast_weights, update_rate, out_gain):
    head_dev = fast_weights.shape[0]
    width = fast_weights.shape[2]
    count_mat = 3 * head_dev
    total_heads = head_dev * lax.axis_size("head")
    weights = fast_weights
    results = []
    for block_idx in range(queries.shape[0]):
        key_blk = key_input[block_idx]
        w_bf = weights.astype(jnp.bfloat16)
        gate_pre = jnp.einsum(
            "nhd,hde->hne", key_blk, w_bf[:, 0], preferred_element_type=jnp.float32
        )
        up_pre = jnp.einsum("nhd,hde->hne", key_blk, w_bf[:, 2], preferred_element_type=jnp.float32)
        sigmoid_gate = jax.nn.sigmoid(gate_pre)
        activated = gate_pre * sigmoid_gate
        hidden = (activated * up_pre).astype(jnp.bfloat16)
        rate_cols = jnp.transpose(token_rates[block_idx])
        target = (-rate_cols[:, :, None] * value_input[block_idx].astype(jnp.float32)).astype(
            jnp.bfloat16
        )
        grad_down = jnp.einsum("hne,nhd->hed", hidden, target, preferred_element_type=jnp.float32)
        back_prop = jnp.einsum(
            "nhd,hed->hne", target, w_bf[:, 1], preferred_element_type=jnp.float32
        )
        up_cot = (back_prop * activated).astype(jnp.bfloat16)
        gate_cot = (
            back_prop * up_pre * sigmoid_gate * (1.0 + gate_pre * (1.0 - sigmoid_gate))
        ).astype(jnp.bfloat16)
        grad_gate = jnp.einsum(
            "nhd,hne->hde", key_blk, gate_cot, preferred_element_type=jnp.float32
        )
        grad_up = jnp.einsum("nhd,hne->hde", key_blk, up_cot, preferred_element_type=jnp.float32)
        grads = jnp.stack([grad_gate, grad_down, grad_up], axis=1)
        total = lax.psum(grads, "tok").reshape(count_mat, width, width)
        norms = jnp.sum(total * total, axis=(1, 2))
        start_iter = (total * lax.rsqrt(norms + 1e-06)[:, None, None]).astype(jnp.bfloat16)
        iterate = lax.optimization_barrier(start_iter)
        for step_idx in range(NS_STEPS):
            gram = lax.optimization_barrier(
                jnp.einsum(
                    "mij,mkj->mik", iterate, iterate, preferred_element_type=jnp.float32
                ).astype(jnp.bfloat16)
            )
            squared = jnp.einsum("mij,mjk->mik", gram, gram, preferred_element_type=jnp.float32)
            poly = (coef_b * gram.astype(jnp.float32) + coef_c * squared).astype(jnp.bfloat16)
            product = jnp.einsum("mij,mjk->mik", poly, iterate, preferred_element_type=jnp.float32)
            iterate = lax.optimization_barrier(
                (coef_a * iterate.astype(jnp.float32) + product).astype(jnp.bfloat16)
            )
        weights = weights - update_rate[:, :, None, None] * iterate.reshape(
            head_dev, 3, width, width
        ).astype(jnp.float32)
        w_bf = weights.astype(jnp.bfloat16)
        query_blk = queries[block_idx]
        gate_query = jnp.einsum(
            "nhd,hde->hne", query_blk, w_bf[:, 0], preferred_element_type=jnp.float32
        )
        up_query = jnp.einsum(
            "nhd,hde->hne", query_blk, w_bf[:, 2], preferred_element_type=jnp.float32
        )
        hidden_query = (gate_query * jax.nn.sigmoid(gate_query) * up_query).astype(jnp.bfloat16)
        mapped = jnp.einsum(
            "hne,hed->nhd", hidden_query, w_bf[:, 1], preferred_element_type=jnp.float32
        )
        squares = lax.psum(jnp.sum(mapped * mapped, axis=(1, 2)), "head")
        scale_rows = lax.rsqrt(squares / (total_heads * width) + 1e-06)
        normed = mapped * scale_rows[:, None, None] * out_gain[None, :, :]
        results.append(normed.astype(jnp.bfloat16))
    return jnp.stack(results)


def solution(mesh):
    return jax.shard_map(
        per_device,
        mesh=mesh,
        in_specs=(
            P(None, "tok", "head", None),
            P(None, "tok", "head", None),
            P(None, "tok", "head", None),
            P(None, "head", "tok"),
            P("head", None, None, None),
            P("head", None),
            P("head", None),
        ),
        out_specs=P(None, "tok", "head", None),
        check_vma=False,
    )
```

profile of v0, /device:TPU:1, one launch (start us, length us, event | category | flops | bytes accessed | tf_op | source)
XLA Modules:
  0.0 518.7 jit_solution(4329020242161983321)
XLA Ops:
  10.5 2.6 fusion.26
  20.4 2.4 copy.82
  22.9 192.1 %all-reduce.4.cloned.1.call-done = f32[4,3,256,256]{2,3,0,1:T(8,128)} async-done(((f32[4,3,256,256]{2,3,0,1:T(8,128)}), f32[4,3,256,256]{2,3,0,1:T(8,128)}) %all-reduce.4.cloned.1.call-update) | async-done | bytes 3145744 | tf_op jit(solution)/shard_map/psum | solution.py:48
  217.4 3.6 copy.79
  226.2 5.7 %add_convert_fusion.10 = bf16[12,256,256]{2,1,0:T(8,128)(2,1)} fusion(bf16[12,256,256]{2,1,0:T(8,128)(2,1)} %copy-done, bf16[12,256,256]{2,1,0:T(8,128)(2,1)} %convolution_convert_fusion.5), kind=kOutput, calls=%fused_computation.20 | convolution fusion | flops 812384256 | bytes 4718592 | tf_op jit(solution)/shard_map/mij,mjk->mik/dot_general | solution.py:60
  231.9 3.6 convolution_convert_fusion.4
  235.5 5.9 %add_convert_fusion.8 = bf16[12,256,256]{2,1,0:T(8,128)(2,1)} fusion(bf16[12,256,256]{2,1,0:T(8,128)(2,1)} %add_convert_fusion.10, bf16[12,256,256]{2,1,0:T(8,128)(2,1)} %convolution_convert_fusion.4), kind=kOutput, calls=%fused_computation.18 | convolution fusion | flops 812384256 | bytes 4718592 | tf_op jit(solution)/shard_map/mij,mjk->mik/dot_general | solution.py:60
  241.4 3.6 convolution_convert_fusion.3
  245.0 5.7 %add_convert_fusion.6 = bf16[12,256,256]{2,1,0:T(8,128)(2,1)} fusion(bf16[12,256,256]{2,1,0:T(8,128)(2,1)} %add_convert_fusion.8, bf16[12,256,256]{2,1,0:T(8,128)(2,1)} %convolution_convert_fusion.3), kind=kOutput, calls=%fused_computation.16 | convolution fusion | flops 812384256 | bytes 4718592 | tf_op jit(solution)/shard_map/mij,mjk->mik/dot_general | solution.py:60
  250.7 3.0 copy.81
  253.8 2.6 fusion.8
  262.1 2.4 fusion.59
  267.6 3.3 multiply_reduce_fusion.3
  270.9 182.2 %all-reduce.6.cloned.1.call-done = f32[4,3,256,256]{2,3,0,1:T(8,128)} async-done(((f32[4,3,256,256]{2,3,0,1:T(8,128)}), f32[4,3,256,256]{2,3,0,1:T(8,128)}) %all-reduce.6.cloned.1.call-update) | async-done | bytes 3145744 | tf_op jit(solution)/shard_map/psum | solution.py:48
  455.5 3.8 copy.97
  464.5 5.8 %add_convert_fusion.4 = bf16[12,256,256]{2,1,0:T(8,128)(2,1)} fusion(bf16[12,256,256]{2,1,0:T(8,128)(2,1)} %copy-done.1, bf16[12,256,256]{2,1,0:T(8,128)(2,1)} %convolution_convert_fusion.2), kind=kOutput, calls=%fused_computation.12 | convolution fusion | flops 812384256 | bytes 4718592 | tf_op jit(solution)/shard_map/mij,mjk->mik/dot_general | solution.py:60
  470.3 3.6 convolution_convert_fusion.1
  473.9 5.7 %add_convert_fusion.2 = bf16[12,256,256]{2,1,0:T(8,128)(2,1)} fusion(bf16[12,256,256]{2,1,0:T(8,128)(2,1)} %add_convert_fusion.4, bf16[12,256,256]{2,1,0:T(8,128)(2,1)} %convolution_convert_fusion.1), kind=kOutput, calls=%fused_computation.10 | convolution fusion | flops 812384256 | bytes 4718592 | tf_op jit(solution)/shard_map/mij,mjk->mik/dot_general | solution.py:60
  479.6 3.7 convolution_convert_fusion
  483.3 5.9 %add_convert_fusion = bf16[12,256,256]{2,1,0:T(8,128)(2,1)} fusion(bf16[12,256,256]{2,1,0:T(8,128)(2,1)} %add_convert_fusion.2, bf16[12,256,256]{2,1,0:T(8,128)(2,1)} %convolution_convert_fusion), kind=kOutput, calls=%fused_computation.8 | convolution fusion | flops 812384256 | bytes 4718592 | tf_op jit(solution)/shard_map/mij,mjk->mik/dot_general | solution.py:60
  489.2 3.1 copy.99
  492.3 3.7 subtract_convert_fusion
  497.6 2.9 multiply_reduce_fusion.2
  500.4 8.4 %all-reduce = (f32[256]{0:T(256)S(1)}, f32[256]{0:T(256)S(1)}) all-reduce(f32[256]{0:T(256)S(1)} %get-tuple-element.17, f32[256]{0:T(256)S(1)} %get-tuple-element.19), channel_id=1, replica_groups=mesh['tok'=64,'head'=4] {'head'}, use_global_device_ids=true, to_apply=%region_7.0 | all-reduce | flops 512 | bytes 4096 | tf_op jit(solution)/shard_map/psum | solution.py:79
  (71 shorter events, 39.8 us)
Async XLA Ops:
  6.5 208.5 %all-reduce.4.cloned.1.call-start = ((), (), s32[]{:S(2)}) async-start(), calls=%async_computation | async-start | bytes 6291456 | tf_op jit(solution)/shard_map/psum | solution.py:48
  8.9 4.2 copy-start.12
  10.4 2.9 copy-start.9
  14.8 1.7 copy-start.11
  20.2 2.6 copy-start.14
  20.2 432.9 %all-reduce.6.cloned.1.call-start = ((), (), s32[]{:S(2)}) async-start(), calls=%async_computation.1 | async-start | bytes 6291456 | tf_op jit(solution)/shard_map/psum | solution.py:48
  223.3 1.1 copy-start
  253.8 2.6 copy-start.3
  256.3 1.2 copy-start.2
  256.7 1.2 copy-start.5
  264.5 0.8 copy-start.8
  461.6 1.2 copy-start.1
  492.3 4.9 copy-start.6
  496.0 1.1 copy-start.4
  496.1 1.5 copy-start.7
  497.5 11.3 %copy-start.10 = (f32[4,256,256]{2,1,0:T(8,128)S(1)}, f32[4,256,256]{2,1,0:T(8,128)}, u32[]{:S(2)}) copy-start(f32[4,256,256]{2,1,0:T(8,128)} %get-tuple-element.20) | copy-start | bytes 3145732
  497.6 11.3 %copy-start.13 = (f32[4,256]{1,0:T(4,128)S(1)}, f32[4,256]{1,0:T(4,128)}, u32[]{:S(2)}) copy-start(f32[4,256]{1,0:T(4,128)} %param.13) | copy-start | bytes 12292
Sparse Core Ops, SparseCore 0:
  20.3 194.6 all-reduce.3
  262.2 190.8 all-reduce.5
where the time goes:
time: 522 us; the launch traced here: 519 us
  waiting for transfers between devices  374 us (72%)
  matrix products  71.9 us (14%)
  local copies, waits for them, and re-layouts  27.9 us (5%)
  other arithmetic  22.3 us (4%)
  between operations  13.7 us (3%)
  blocking collectives  8.4 us (2%)
    psum x2, waiting for transfers between devices, per_device(): total = lax.psum(grads, 'tok').reshape(count_mat, width, width)  374 us
    dot_general x6, matrix products, per_device(): jnp.einsum('mij,mjk->mik', poly, iterate, preferred_element_type=jnp.floa...  34.7 us
    dot_general x6, matrix products, per_device(): jnp.einsum('mij,mkj->mik', iterate, iterate, preferred_element_type=jnp.f...  18.1 us
  transfers between devices with their start and end apart: 2, of which 2 were waited for; matrix products, arithmetic and copies ran while one was open for 2% of the time, Pallas kernels for 0%

commit v1 on v0

v1 whole, which is shorter than its diff:
```python
import functools

import jax
import jax.numpy as jnp
from jax import lax
from jax.experimental import pallas as pl
from jax.experimental.pallas import tpu as pltpu
from jax.sharding import PartitionSpec as P

NS_STEPS = 3
SIZE_Y = 4

coef_a = 3.4445
coef_b = -4.775
coef_c = 2.0315

BF = jnp.bfloat16
F32 = jnp.float32
MESH = pl.DeviceIdType.MESH
KEY, TGT, QRY = 0, 1, 2

ROUTES = (
    (0, 1, 1, 0, 128, 256),
    (0, -1, 1, 128, 128, 384),
    (1, 0, 2, 0, 128, 512),
    (-1, 0, 2, 128, 128, 640),
    (1, 1, 3, 0, 64, 768),
    (1, -1, 3, 64, 64, 832),
    (-1, 1, 3, 128, 64, 896),
    (-1, -1, 3, 192, 64, 960),
)


def mm(a, b):
    return jnp.dot(a, b, preferred_element_type=F32)


def mm_nt(a, b):
    return lax.dot_general(a, b, (((1,), (1,)), ((), ())), preferred_element_type=F32)


def mm_tn(a, b):
    return lax.dot_general(a, b, (((0,), (0,)), ((), ())), preferred_element_type=F32)


def kernel(
    size_z, size_x,
    q_hbm, k_hbm, v_hbm, rate_ref, w_hbm, lr_ref, gain_ref, out_hbm,
    raw, raw_out, moved, staged, weights, weights_bf, hid, gate_cot, up_cot, grads,
    pair_src, pair_dst, half, ring_src, ring_dst, full, map_src, map_dst, tile_buf, sq_src, sq_dst,
    load_sem, w_sem, store_sem, move_s, move_r, pair_s, pair_r, ring_s, ring_r, all_s, all_r,
    twin_s, twin_r, back_s, back_r, sq_s, sq_r,
):
    bits_z = size_z.bit_length() - 1
    half_y, half_z = SIZE_Y // 2, size_z // 2
    members = half_y * half_z
    piece = 128 // members
    total_heads = 4 * size_x
    tok = lax.axis_index("tok")
    head_x = lax.axis_index("head")
    core = tok & 1
    z = (tok >> 1) & (size_z - 1)
    y = tok >> (1 + bits_z)
    own = 2 * (y & 1) + (z & 1)
    group = (y >> 1) * half_z + (z >> 1)

    def chip(dy, dz, dc=0):
        at_y = (y + dy) & (SIZE_Y - 1)
        at_z = (z + dz) & (size_z - 1)
        return {"tok": (at_y * size_z + at_z) * 2 + (core ^ dc)}

    def across(step):
        return {"head": (head_x + step) & (size_x - 1)}

    peers = [(i, j) for i in range(half_y) for j in range(half_z) if i + j > 0]

    sources = {KEY: k_hbm, TGT: v_hbm, QRY: q_hbm}

    def load(kind, b):
        return pltpu.make_async_copy(sources[kind].at[b], raw.at[kind, b], load_sem.at[kind, b])

    load(KEY, 0).start()
    load(TGT, 0).start()
    w_load = pltpu.make_async_copy(w_hbm.at[own], weights, w_sem)
    w_load.start()
    for kind, b in ((KEY, 1), (TGT, 1), (QRY, 0), (QRY, 1)):
        load(kind, b).start()

    barrier = pltpu.get_barrier_semaphore()
    greeted = [chip(dy, dz) for dy, dz, *_ in ROUTES]
    greeted += [chip(2 * i, 2 * j) for i, j in peers]
    greeted += [chip(0, 0, 1)]
    greeted += [across(s) for s in range(1, size_x)]
    for device in greeted:
        pl.semaphore_signal(barrier, inc=1, device_id=device, device_id_type=MESH)

    rows_i = lax.broadcasted_iota(jnp.int32, (256, 256), 0)
    cols_i = lax.broadcasted_iota(jnp.int32, (256, 256), 1)

    def source_row(i):
        return (i & 31) * 8 + ((i >> 5) & 1) * 4 + ((i >> 6) ^ own)

    gather = jnp.where(source_row(rows_i) == cols_i, 1.0, 0.0).astype(BF)
    scatter = jnp.where(source_row(cols_i) == rows_i, 1.0, 0.0).astype(BF)

    def split_heads(kind, b):
        load(kind, b).wait()
        if kind == TGT:
            rates = []
            for r in range(4):
                row = rate_ref[b, pl.ds(r ^ own, 1), :]
                rates.append(-jnp.transpose(jnp.broadcast_to(row, (128, 256))))
        for g in range(4):
            lo = raw[kind, b, 512 * g : 512 * g + 256, :]
            hi = raw[kind, b, 512 * g + 256 : 512 * g + 512, :]
            out = mm(gather, jnp.concatenate([lo, hi], axis=1))
            for r in range(4):
                for c in range(2):
                    for k in range(2):
                        t = 64 * g + 32 * k
                        tile = out[64 * r + 32 * c : 64 * r + 32 * c + 32, 128 * k : 128 * k + 128]
                        if kind == TGT:
                            tile = tile * rates[r][t : t + 32, :]
                        tile = tile.astype(BF)
                        cols = slice(128 * c, 128 * c + 128)
                        if r == 0:
                            moved[b, kind, t : t + 32, cols] = tile
                        else:
                            staged[b, kind, r - 1, t : t + 32, cols] = tile

    def remote(src, dst, s, r, device):
        return pltpu.make_async_remote_copy(
            src_ref=src, dst_ref=dst, send_sem=s, recv_sem=r, device_id=device, device_id_type=MESH
        )

    def send_moved(kind, b):
        for dy, dz, r, t, n, row in ROUTES:
            remote(
                staged.at[b, kind, r - 1, pl.ds(t, n)],
                moved.at[b, kind, pl.ds(row, n)],
                move_s.at[b, kind], move_r.at[b, kind], chip(dy, dz),
            ).start()

    def moved_all(kind, b):
        return remote(
            staged.at[b, kind], staged.at[b, kind], move_s.at[b, kind], move_r.at[b, kind], chip(0, 1)
        )

    def gradients(b):
        for i in range(4):
            rows = slice(256 * i, 256 * i + 256)
            key = moved[b, KEY, rows, :]
            gate_pre = mm(key, weights_bf[0])
            up_pre = mm(key, weights_bf[2])
            back = mm_nt(moved[b, TGT, rows, :], weights_bf[1])
            sg = jax.nn.sigmoid(gate_pre)
            act = gate_pre * sg
            hid[rows, :] = (act * up_pre).astype(BF)
            up_cot[rows, :] = (back * act).astype(BF)
            gate_cot[rows, :] = (back * up_pre * sg * (1.0 + gate_pre * (1.0 - sg))).astype(BF)
        grads[0] = mm_tn(moved[b, KEY], gate_cot[...])
        grads[1] = mm_tn(hid[...], moved[b, TGT])
        grads[2] = mm_tn(moved[b, KEY], up_cot[...])

    def pair_copy(b):
        return remote(pair_src.at[b], pair_dst.at[b], pair_s.at[b], pair_r.at[b], chip(0, 0, 1))

    def send_pair(b):
        other = pl.multiple_of((1 - core) * 128, 128)
        pair_src[b] = grads[:, pl.ds(other, 128), :].astype(BF)
        pair_copy(b).start()

    def ring_all(b):
        return remote(ring_dst.at[b], ring_dst.at[b], ring_s.at[b], ring_r.at[b], chip(0, 2))

    def send_ring(b):
        mine = pl.multiple_of(core * 128, 128)
        pair_copy(b).wait_recv()
        total = grads[:, pl.ds(mine, 128), :] + pair_dst[b].astype(F32)
        half[...] = total
        ring_src[b] = total.astype(BF)
        for k, (i, j) in enumerate(peers):
            there = (((y >> 1) + i) & (half_y - 1)) * half_z + (((z >> 1) + j) & (half_z - 1))
            rows = pl.ds(pl.multiple_of(there * piece, piece), piece)
            remote(
                ring_src.at[b, :, rows, :], ring_dst.at[b, k], ring_s.at[b], ring_r.at[b], chip(2 * i, 2 * j)
            ).start()

    def all_all(b):
        return remote(ring_dst.at[b], ring_dst.at[b], all_s.at[b], all_r.at[b], chip(0, 2))

    def send_all(b):
        ring_all(b).wait_recv()
        total = half[:, pl.ds(pl.multiple_of(group * piece, piece), piece), :]
        for k in range(len(peers)):
            total = total + ring_dst[b, k].astype(F32)
        rows = pl.ds(pl.multiple_of(core * 128 + group * piece, piece), piece)
        full[b, :, rows, :] = total.astype(BF)
        for i, j in peers:
            remote(
                full.at[b, :, rows, :], full.at[b, :, rows, :], all_s.at[b], all_r.at[b], chip(2 * i, 2 * j)
            ).start()

    def twin_copy(b):
        rows = pl.ds(pl.multiple_of(core * 128, 128), 128)
        return remote(full.at[b, :, rows, :], full.at[b, :, rows, :], twin_s.at[b], twin_r.at[b], chip(0, 0, 1))

    def send_twin(b):
        all_all(b).wait_recv()
        twin_copy(b).start()

    def update(b):
        xs, inverse = [], []
        for m in range(3):
            x = full[b, m]
            xf = x.astype(F32)
            xs.append(x)
            inverse.append(lax.rsqrt(jnp.sum(xf * xf, keepdims=True) + 1e-06))
        for step in range(NS_STEPS):
            grams = []
            for m in range(3):
                gram = mm_nt(xs[m], xs[m])
                if step == 0:
                    gram = gram * inverse[m] * inverse[m]
                grams.append(gram.astype(BF))
            polys = [
                (coef_b * grams[m].astype(F32) + coef_c * mm(grams[m], grams[m])).astype(BF) for m in range(3)
            ]
            for m in range(3):
                x = coef_a * xs[m].astype(F32) + mm(polys[m], xs[m])
                if step == 0:
                    x = x * inverse[m]
                xs[m] = x.astype(BF)
        for m in range(3):
            new = weights[m] - lr_ref[own, m] * xs[m].astype(F32)
            weights[m] = new
            weights_bf[m] = new.astype(BF)

    def apply(b):
        for i in range(4):
            rows = slice(256 * i, 256 * i + 256)
            query = moved[b, QRY, rows, :]
            gate = mm(query, weights_bf[0])
            up = mm(query, weights_bf[2])
            mapped = mm((gate * jax.nn.sigmoid(gate) * up).astype(BF), weights_bf[1]).astype(BF)
            if i == 0:
                map_dst[b, 0] = mapped
            else:
                map_src[b, i - 1] = mapped

    def send_back(b):
        for dy, dz, r, t, n, row in ROUTES:
            at = row - 256
            remote(
                map_src.at[b, at // 256, pl.ds(at % 256, n)],
                map_dst.at[b, r, pl.ds(t, n)],
                back_s.at[b], back_r.at[b], chip(-dy, -dz),
            ).start()

    def back_all(b):
        return remote(map_src.at[b], map_src.at[b], back_s.at[b], back_r.at[b], chip(0, 1))

    def squares_all(b):
        return remote(sq_dst.at[b], sq_dst.at[b], sq_s.at[b], sq_r.at[b], across(1))

    def send_squares(b):
        back_all(b).wait_recv()
        squares = jnp.zeros((256, 256), F32)
        for r in range(4):
            part = map_dst[b, r].astype(F32)
            squares = squares + part * part
        high = squares.astype(BF)
        low = (squares - high.astype(F32)).astype(BF)
        ones = jnp.ones((8, 256), BF)
        sq_src[b] = mm_nt(ones, high) + mm_nt(ones, low)
        for s in range(1, size_x):
            remote(sq_src.at[b], sq_dst.at[b, s - 1], sq_s.at[b], sq_r.at[b], across(s)).start()

    def store(b):
        return pltpu.make_async_copy(raw_out.at[b], out_hbm.at[b], store_sem.at[b])

    def finish(b):
        total = sq_src[b]
        if size_x > 1:
            squares_all(b).wait_recv()
            for s in range(1, size_x):
                total = total + sq_dst[b, s - 1]
        scale = lax.rsqrt(total * (1.0 / (total_heads * 256)) + 1e-06)
        scale = jnp.transpose(jnp.broadcast_to(scale[0:1, :], (128, 256)))
        gains = [gain_ref[pl.ds(r ^ own, 1), :] for r in range(4)]
        for g in range(4):
            for r in range(4):
                for c in range(2):
                    for k in range(2):
                        t = 64 * g + 32 * k
                        cols = slice(128 * c, 128 * c + 128)
                        tile = map_dst[b, r, t : t + 32, cols].astype(F32) * scale[t : t + 32, :]
                        tile = tile * gains[r][:, cols]
                        tile_buf[g, 64 * r + 32 * c : 64 * r + 32 * c + 32, 128 * k : 128 * k + 128] = tile.astype(BF)
        for g in range(4):
            out = mm(scatter, tile_buf[g]).astype(BF)
            raw_out[b, 512 * g : 512 * g + 256, :] = out[:, :128]
            raw_out[b, 512 * g + 256 : 512 * g + 512, :] = out[:, 128:]
        store(b).start()

    split_heads(KEY, 0)
    pl.semaphore_wait(barrier, len(greeted))
    send_moved(KEY, 0)
    split_heads(TGT, 0)
    send_moved(TGT, 0)
    w_load.wait()
    weights_bf[...] = weights[...].astype(BF)
    split_heads(KEY, 1)
    split_heads(TGT, 1)
    split_heads(QRY, 0)
    split_heads(QRY, 1)
    moved_all(KEY, 0).wait_recv()
    moved_all(TGT, 0).wait_recv()
    gradients(0)
    send_pair(0)
    send_moved(KEY, 1)
    send_moved(TGT, 1)
    send_ring(0)
    send_all(0)
    send_twin(0)
    send_moved(QRY, 0)
    send_moved(QRY, 1)
    twin_copy(0).wait_recv()
    update(0)
    moved_all(KEY, 1).wait_recv()
    moved_all(TGT, 1).wait_recv()
    gradients(1)
    send_pair(1)
    send_ring(1)
    moved_all(QRY, 0).wait_recv()
    apply(0)
    send_all(1)
    send_twin(1)
    send_back(0)
    twin_copy(1).wait_recv()
    update(1)
    moved_all(QRY, 1).wait_recv()
    apply(1)
    send_back(1)
    send_squares(0)
    finish(0)
    send_squares(1)
    finish(1)
    for b in range(2):
        for kind in (KEY, TGT, QRY):
            moved_all(kind, b).wait_send()
        pair_copy(b).wait_send()
        ring_all(b).wait_send()
        all_all(b).wait_send()
        twin_copy(b).wait_send()
        back_all(b).wait_send()
        if size_x > 1:
            squares_all(b).wait_send()
        store(b).wait()


def per_device(size_z, size_x, queries, key_input, value_input, token_rates, fast_weights, update_rate, out_gain):
    members = (SIZE_Y // 2) * (size_z // 2)
    piece = 128 // members

    def flat(a):
        return a.reshape(2, 256, 4, 2, 128).transpose(0, 1, 3, 2, 4).reshape(2, 2048, 128)

    vmem = pl.BlockSpec(memory_space=pltpu.VMEM)
    smem = pl.BlockSpec(memory_space=pltpu.SMEM)
    hbm = pl.BlockSpec(memory_space=pl.ANY)
    dma = pltpu.SemaphoreType.DMA
    out = pl.pallas_call(
        functools.partial(kernel, size_z, size_x),
        out_shape=jax.ShapeDtypeStruct((2, 2048, 128), BF),
        in_specs=[hbm, hbm, hbm, vmem, hbm, smem, vmem],
        out_specs=hbm,
        scratch_shapes=[
            pltpu.VMEM((3, 2, 2048, 128), BF),
            pltpu.VMEM((2, 2048, 128), BF),
            pltpu.VMEM((2, 3, 1024, 256), BF),
            pltpu.VMEM((2, 3, 3, 256, 256), BF),
            pltpu.VMEM((3, 256, 256), F32),
            pltpu.VMEM((3, 256, 256), BF),
            pltpu.VMEM((1024, 256), BF),
            pltpu.VMEM((1024, 256), BF),
            pltpu.VMEM((1024, 256), BF),
            pltpu.VMEM((3, 256, 256), F32),
            pltpu.VMEM((2, 3, 128, 256), BF),
            pltpu.VMEM((2, 3, 128, 256), BF),
            pltpu.VMEM((3, 128, 256), F32),
            pltpu.VMEM((2, 3, 128, 256), BF),
            pltpu.VMEM((2, members - 1, 3, piece, 256), BF),
            pltpu.VMEM((2, 3, 256, 256), BF),
            pltpu.VMEM((2, 3, 256, 256), BF),
            pltpu.VMEM((2, 4, 256, 256), BF),
            pltpu.VMEM((4, 256, 256), BF),
            pltpu.VMEM((2, 8, 256), F32),
            pltpu.VMEM((2, max(size_x - 1, 1), 8, 256), F32),
            dma((3, 2)), dma, dma((2,)),
            dma((2, 3)), dma((2, 3)),
            *[dma((2,)) for _ in range(12)],
        ],
        compiler_params=pltpu.CompilerParams(
            collective_id=0, has_side_effects=True, vmem_limit_bytes=48 * 1024 * 1024
        ),
        cost_estimate=pl.CostEstimate(flops=12_000_000_000, bytes_accessed=5_000_000, transcendentals=1_000_000),
    )(flat(queries), flat(key_input), flat(value_input), token_rates, fast_weights, update_rate, out_gain)
    return out.reshape(2, 256, 2, 4, 128).transpose(0, 1, 3, 2, 4).reshape(2, 256, 4, 256)


def solution(mesh):
    size_z = mesh.shape["tok"] // (2 * SIZE_Y)
    return jax.shard_map(
        functools.partial(per_device, size_z, mesh.shape["head"]),
        mesh=mesh,
        in_specs=(
            P(None, "tok", "head", None),
            P(None, "tok", "head", None),
            P(None, "tok", "head", None),
            P(None, "head", "tok"),
            P("head", None, None, None),
            P("head", None),
            P("head", None),
        ),
        out_specs=P(None, "tok", "head", None),
        check_vma=False,
    )
```

time: 522 us -> 84.4 us (0.16)
  waiting for transfers between devices: 374 us -> 0 us
  Pallas kernels: 0 us -> 77.4 us
  matrix products: 71.9 us -> 0 us
  other arithmetic: 22.3 us -> 0 us
  local copies, waits for them, and re-layouts: 27.9 us -> 6.71 us
  between operations: 13.7 us -> 0.02 us
  blocking collectives: 8.4 us -> 0 us
    psum x2 -> x0, waiting for transfers between devices: 374 us -> none  [per_device(): total = lax.psum(grads, 'tok').reshape(count_mat, width, width)]
    pallas_call x0 -> x1, Pallas kernels: none -> 77.4 us  [per_device(): pl.pallas_call(functools.partial(kernel, size_z, size_x), out_shape=jax.S...]
    dot_general x28 -> x0, matrix products: 71.9 us -> none  [the longest x6 34.7 us: per_device(): jnp.einsum('mij,mjk->mik', poly, iterate, preferred_element_type=jnp.floa...]
    convert_element_type x5 -> x0, other arithmetic: 12.2 us -> none  [the longest x2 6.27 us: per_device(): w_bf = weights.astype(jnp.bfloat16)]
    psum x1 -> x0, blocking collectives: 8.4 us -> none  [per_device(): squares = lax.psum(jnp.sum(mapped * mapped, axis=(1, 2)), 'head')]
    psum x2 -> x0, local copies, waits for them, and re-layouts: 7.33 us -> none  [per_device(): total = lax.psum(grads, 'tok').reshape(count_mat, width, width)]
    convert_element_type x2 -> x0, local copies, waits for them, and re-layouts: 6.12 us -> none  [per_device(): weights = weights - update_rate[:, :, None, None] * iterate.reshape(head_...]
    another operation x4 -> x0, other arithmetic: 5.69 us -> none  [the longest x2 4.11 us: per_device(): grads = jnp.stack([grad_gate, grad_down, grad_up], axis=1)]
  transfers between devices with their start and end apart: 2 -> 0, of which waited for: 2 -> 0; matrix products, arithmetic and copies ran while one was open for 2% -> 0% of each run, Pallas kernels for 0% -> 0%
where the time goes in v1:
time: 84.4 us; the launch traced here: 84.2 us
  Pallas kernels  77.4 us (92%)
  local copies, waits for them, and re-layouts  6.71 us (8%)
    pallas_call x1, Pallas kernels, per_device(): pl.pallas_call(functools.partial(kernel, size_z, size_x), out_shape=jax.S...  77.4 us
    unnamed x13, local copies, waits for them, and re-layouts  6.71 us

profile of v1, /device:TPU:1, one launch (start us, length us, event | category | flops | bytes accessed | tf_op | source)
XLA Modules:
  0.0 84.2 jit_solution(11731928338939595977)
XLA Ops:
  0.0 0.0 copy-start
  0.0 1.2 %copy-done = bf16[2,256,4,256]{3,2,1,0:T(4,128)(2,1)S(1)} copy-done((bf16[2,256,4,256]{3,2,1,0:T(4,128)(2,1)S(1)}, bf16[2,256,4,256]{3,2,1,0:T(4,128)(2,1)}, u32[]{:S(2)}) %copy-start) | copy-done | bytes 1048600
  1.2 0.0 copy-start.1
  1.2 1.2 %copy-done.1 = bf16[2,256,4,256]{3,2,1,0:T(4,128)(2,1)S(1)} copy-done((bf16[2,256,4,256]{3,2,1,0:T(4,128)(2,1)S(1)}, bf16[2,256,4,256]{3,2,1,0:T(4,128)(2,1)}, u32[]{:S(2)}) %copy-start.1) | copy-done | bytes 1048600
  2.5 0.0 copy-start.2
  2.5 1.2 %copy-done.2 = bf16[2,256,4,256]{3,2,1,0:T(4,128)(2,1)S(1)} copy-done((bf16[2,256,4,256]{3,2,1,0:T(4,128)(2,1)S(1)}, bf16[2,256,4,256]{3,2,1,0:T(4,128)(2,1)}, u32[]{:S(2)}) %copy-start.2) | copy-done | bytes 1048600
  3.7 0.0 copy-start.3
  3.7 0.7 copy-done.3
  4.4 0.0 copy-start.4
  4.4 0.7 copy-done.4
  5.1 0.0 copy-start.5
  5.1 0.7 copy-done.5
  5.7 77.4 %shard_map.73 = bf16[2,2048,128]{2,1,0:T(8,128)(2,1)S(1)} custom-call(bf16[2,2048,128]{2,1,0:T(8,128)(2,1)S(1)} %bitcast.21, bf16[2,2048,128]{2,1,0:T(8,128)(2,1)S(1)} %bitcast.22, bf16[2,2048,128]{2,1,0:T(8,128)(2,1)S(1)} %bitcast.23, f32[2,4,256]{2,1,0:T(4,128)S(1)} %copy-done.3, f32[4,3,256,256]{3,2,1,0:T(8,128)} %w_hbm.1, f32[4,3]{1,0:T(4,128)S(1)} %copy-done.5, ...), custom_call_target="tpu_custom_call" | custom-call | flops 12000000000 | bytes 5000000 | tf_op jit(solution)/shard_map/pallas_call | solution.py:373
  83.2 1.0 %copy.13 = bf16[2,256,4,256]{3,2,1,0:T(4,128)(2,1)} copy(bf16[2,256,4,256]{3,2,1,0:T(4,128)(2,1)S(1)} %bitcast.20) | data formatting | bytes 2097152
Async XLA Ops:
  0.0 1.2 %copy-start = (bf16[2,256,4,256]{3,2,1,0:T(4,128)(2,1)S(1)}, bf16[2,256,4,256]{3,2,1,0:T(4,128)(2,1)}, u32[]{:S(2)}) copy-start(bf16[2,256,4,256]{3,2,1,0:T(4,128)(2,1)} %param.7) | copy-start | bytes 3145732
  1.2 1.2 %copy-start.1 = (bf16[2,256,4,256]{3,2,1,0:T(4,128)(2,1)S(1)}, bf16[2,256,4,256]{3,2,1,0:T(4,128)(2,1)}, u32[]{:S(2)}) copy-start(bf16[2,256,4,256]{3,2,1,0:T(4,128)(2,1)} %param.8) | copy-start | bytes 3145732
  2.5 1.2 %copy-start.2 = (bf16[2,256,4,256]{3,2,1,0:T(4,128)(2,1)S(1)}, bf16[2,256,4,256]{3,2,1,0:T(4,128)(2,1)}, u32[]{:S(2)}) copy-start(bf16[2,256,4,256]{3,2,1,0:T(4,128)(2,1)} %param.9) | copy-start | bytes 3145732
  3.7 0.7 copy-start.3
  4.4 0.7 copy-start.4
  5.1 0.7 copy-start.5

commit v2 on v1

v2 whole, which is shorter than its diff:
```python
import functools

import jax
import jax.numpy as jnp
from jax import lax
from jax.experimental import pallas as pl
from jax.experimental.pallas import tpu as pltpu
from jax.sharding import PartitionSpec as P

NS_STEPS = 3
SIZE_Y = 4

coef_a = 3.4445
coef_b = -4.775
coef_c = 2.0315

BF = jnp.bfloat16
F32 = jnp.float32
MESH = pl.DeviceIdType.MESH
KEY, TGT, QRY = 0, 1, 2
HALF = 128

ROUTES = (
    (-1, 1, 2, 0, 768),
    (1, -1, 2, 128, 896),
    (0, 1, 1, 0, 256),
    (-1, 0, 1, 128, 384),
    (0, -1, 3, 0, 512),
    (1, 0, 3, 128, 640),
)


def mm(a, b):
    return jnp.dot(a, b, preferred_element_type=F32)


def mm_nt(a, b):
    return lax.dot_general(a, b, (((1,), (1,)), ((), ())), preferred_element_type=F32)


def mm_tn(a, b):
    return lax.dot_general(a, b, (((0,), (0,)), ((), ())), preferred_element_type=F32)


def kernel(
    size_z, size_x,
    q_hbm, k_hbm, v_hbm, rate_hbm, w_hbm, lr_hbm, gain_hbm, out_hbm,
    raw, rate_ref, lr_ref, gain_ref, raw_out, moved, staged, query, query_staged,
    weights, weights_bf, w_gu, w_down, hid, cots, sums, ring_src, ring_dst, full,
    map_src, map_dst, tile_buf, row_src, row_dst, sq_src, sq_dst,
    load_sem, w_sem, small_sem, store_sem, move_s, move_r, fwd_s, fwd_r, query_s, query_r,
    ring_s, ring_r, all_s, all_r, twin_s, twin_r, row_s, row_r, back_s, back_r, sq_s, sq_r,
):
    bits_z = size_z.bit_length() - 1
    rows_gu, rows_down = 256 // size_z, 128 // size_z
    total_heads = 4 * size_x
    tok = lax.axis_index("tok")
    head_x = lax.axis_index("head")
    core = tok & 1
    z = (tok >> 1) & (size_z - 1)
    y = tok >> (1 + bits_z)
    own = (z - y) & 3

    def chip(dy, dz, dc=0):
        at_y = (y + dy) & (SIZE_Y - 1)
        at_z = (z + dz) & (size_z - 1)
        return {"tok": (at_y * size_z + at_z) * 2 + (core ^ dc)}

    def across(step):
        return {"head": (head_x + step) & (size_x - 1)}

    peers = sorted(range(1, size_z), key=lambda k: abs(k - size_z // 2))

    sources = {KEY: k_hbm, TGT: v_hbm, QRY: q_hbm}

    def load(kind, b):
        return pltpu.make_async_copy(sources[kind].at[b], raw.at[kind, b], load_sem.at[kind, b])

    barrier = pltpu.get_barrier_semaphore()
    greeted = [chip(k, k) for k in peers]
    greeted += [chip(dy, dz) for dy, dz, *_ in ROUTES]
    greeted += [across(s) for s in range(1, size_x)]
    greeted += [chip(0, 0, 1)]
    load(KEY, 0).start()
    load(TGT, 0).start()
    for device in greeted:
        pl.semaphore_signal(barrier, inc=1, device_id=device, device_id_type=MESH)
    w_load = pltpu.make_async_copy(w_hbm.at[own], weights, w_sem)
    small = [
        pltpu.make_async_copy(src, dst, small_sem.at[i])
        for i, (src, dst) in enumerate([(rate_hbm, rate_ref), (lr_hbm, lr_ref), (gain_hbm, gain_ref)])
    ]
    for copy in [small[0], w_load, small[1], small[2]]:
        copy.start()
    for kind, b in ((KEY, 1), (TGT, 1), (QRY, 0), (QRY, 1)):
        load(kind, b).start()

    rows_i = lax.broadcasted_iota(jnp.int32, (256, 256), 0)
    cols_i = lax.broadcasted_iota(jnp.int32, (256, 256), 1)

    def source_row(i):
        return (i & 31) * 8 + ((i >> 5) & 1) * 4 + (((i >> 6) + own) & 3)

    gather = jnp.where(source_row(rows_i) == cols_i, 1.0, 0.0).astype(BF)
    scatter = jnp.where(source_row(cols_i) == rows_i, 1.0, 0.0).astype(BF)

    def split_heads(kind, b):
        load(kind, b).wait()
        if kind == TGT:
            if b == 0:
                small[0].wait()
            rates = []
            for r in range(4):
                row = rate_ref[b, pl.ds((r + own) & 3, 1), :]
                rates.append(-jnp.transpose(jnp.broadcast_to(row, (128, 256))))
        for g in range(4):
            lo = raw[kind, b, 512 * g : 512 * g + 256, :]
            hi = raw[kind, b, 512 * g + 256 : 512 * g + 512, :]
            out = mm(gather, jnp.concatenate([lo, hi], axis=1))
            for r in range(4):
                for c in range(2):
                    for k in range(2):
                        t = 64 * g + 32 * k
                        tile = out[64 * r + 32 * c : 64 * r + 32 * c + 32, 128 * k : 128 * k + 128]
                        if kind == TGT:
                            tile = tile * rates[r][t : t + 32, :]
                        tile = tile.astype(BF)
                        cols = slice(128 * c, 128 * c + 128)
                        if kind == QRY and r == 0:
                            query[b, t : t + 32, cols] = tile
                        elif kind == QRY:
                            query_staged[b, r - 1, t : t + 32, cols] = tile
                        elif r == 0:
                            moved[b, 0, kind, t : t + 32, cols] = tile
                        else:
                            staged[b, kind, r - 1, t : t + 32, cols] = tile

    def remote(src, dst, s, r, device):
        return pltpu.make_async_remote_copy(
            src_ref=src, dst_ref=dst, send_sem=s, recv_sem=r, device_id=device, device_id_type=MESH
        )

    twin = chip(0, 0, 1)

    def moved_piece(b, i):
        dy, dz, r, t, row = ROUTES[i]
        return remote(
            staged.at[b, :, r - 1, pl.ds(t, HALF)],
            moved.at[b, 0, :, pl.ds(row, HALF)],
            move_s.at[b], move_r.at[b, i], chip(dy, dz),
        )

    def send_moved(b):
        for i in range(len(ROUTES)):
            moved_piece(b, i).start()

    def moved_all(b):
        return remote(staged.at[b], staged.at[b], move_s.at[b], move_r.at[b, 0], twin)

    def forward_rows(b, row, n):
        rows = pl.ds(row, n)
        return remote(moved.at[b, 0, :, rows], moved.at[b, 1, :, rows], fwd_s.at[b], fwd_r.at[b], twin)

    def send_own(b):
        forward_rows(b, 0, 256).start()

    def send_forward(b):
        for i in (2, 3, 4, 5, 0, 1):
            moved_piece(b, i).wait_recv()
            forward_rows(b, ROUTES[i][-1], HALF).start()

    def forward_all(b):
        return remote(moved.at[b, 0], moved.at[b, 1], fwd_s.at[b], fwd_r.at[b], twin)

    def send_query(b):
        for dy, dz, r, t, row in ROUTES:
            remote(
                query_staged.at[b, r - 1, pl.ds(t, HALF)], query.at[b, pl.ds(row, HALF)],
                query_s.at[b], query_r.at[b], chip(dy, dz),
            ).start()

    def query_all(b):
        return remote(query_staged.at[b], query_staged.at[b], query_s.at[b], query_r.at[b], twin)

    def gradients(b, s):
        for i in range(4):
            rows = slice(256 * i, 256 * i + 256)
            pre = mm(moved[b, s, KEY, rows, :], w_gu[...])
            gate_pre, up_pre = pre[:, :HALF], pre[:, HALF:]
            back = mm_nt(moved[b, s, TGT, rows, :], w_down[...])
            sg = jax.nn.sigmoid(gate_pre)
            act = gate_pre * sg
            hid[s, rows, :] = (act * up_pre).astype(BF)
            cots[s, rows, :HALF] = (back * up_pre * sg * (1.0 + gate_pre * (1.0 - sg))).astype(BF)
            cots[s, rows, HALF:] = (back * act).astype(BF)
        grad_gu = mm_tn(moved[b, s, KEY], cots[s]).reshape(size_z, rows_gu, 256)
        grad_down = mm_tn(hid[s], moved[b, s, TGT]).reshape(size_z, rows_down, 256)
        if s == 0:
            sums[:, :rows_gu, :] = grad_gu
            sums[:, rows_gu:, :] = grad_down
        else:
            grad_gu = sums[:, :rows_gu, :] + grad_gu
            grad_down = sums[:, rows_gu:, :] + grad_down
            sums[:, :rows_gu, :] = grad_gu
            sums[:, rows_gu:, :] = grad_down
            ring_src[b, :, :rows_gu, :] = grad_gu.astype(BF)
            ring_src[b, :, rows_gu:, :] = grad_down.astype(BF)

    def send_ring(b):
        for k in peers:
            remote(
                ring_src.at[b, (z + k) & (size_z - 1)], ring_dst.at[b, k - 1],
                ring_s.at[b], ring_r.at[b], chip(k, k),
            ).start()

    def ring_all(b):
        return remote(ring_dst.at[b], ring_dst.at[b], ring_s.at[b], ring_r.at[b], twin)

    def send_all(b):
        total = sums[z]
        for k in peers:
            total = total + ring_dst[b, k - 1].astype(F32)
        full[b, core, z] = total.astype(BF)
        for k in peers:
            remote(full.at[b, core, z], full.at[b, core, z], all_s.at[b], all_r.at[b], chip(k, k)).start()

    def all_all(b):
        return remote(ring_dst.at[b], ring_dst.at[b], all_s.at[b], all_r.at[b], twin)

    def twin_copy(b):
        return remote(full.at[b, core], full.at[b, core], twin_s.at[b], twin_r.at[b], twin)

    def send_twin(b):
        twin_copy(b).start()

    def set_weights(m, new):
        wide = new.astype(BF)
        weights_bf[m] = wide
        first = core == 0
        if m == 1:
            w_down[...] = jnp.where(first, new[:HALF, :], new[HALF:, :]).astype(BF)
        else:
            cols = slice(0, HALF) if m == 0 else slice(HALF, 256)
            w_gu[:, cols] = jnp.where(first, new[:, :HALF], new[:, HALF:]).astype(BF)

    def load_weights():
        w_load.wait()
        small[1].wait()
        small[2].wait()
        for m in range(3):
            set_weights(m, weights[m])

    def update(b):
        sides = [full[b, c, :, :rows_gu, :].reshape(256, 256) for c in range(2)]
        xs = [
            jnp.concatenate([side[:, :HALF] for side in sides], axis=1),
            jnp.concatenate([full[b, c, :, rows_gu:, :].reshape(HALF, 256) for c in range(2)], axis=0),
            jnp.concatenate([side[:, HALF:] for side in sides], axis=1),
        ]
        inverse = []
        for m in range(3):
            xf = xs[m].astype(F32)
            inverse.append(lax.rsqrt(jnp.sum(xf * xf, keepdims=True) + 1e-06))
        for step in range(NS_STEPS):
            grams = []
            for m in range(3):
                gram = mm_nt(xs[m], xs[m])
                if step == 0:
                    gram = gram * inverse[m] * inverse[m]
                grams.append(gram.astype(BF))
            polys = [
                (coef_b * grams[m].astype(F32) + coef_c * mm(grams[m], grams[m])).astype(BF) for m in range(3)
            ]
            for m in range(3):
                x = coef_a * xs[m].astype(F32) + mm(polys[m], xs[m])
                if step == 0:
                    x = x * inverse[m]
                xs[m] = x.astype(BF)
        for m in range(3):
            new = weights[m] - lr_ref[own, m] * xs[m].astype(F32)
            weights[m] = new
            set_weights(m, new)

    def apply(b, chunks):
        for i in chunks:
            rows = slice(256 * i, 256 * i + 256)
            gate = mm(query[b, rows, :], weights_bf[0])
            up = mm(query[b, rows, :], weights_bf[2])
            mapped = mm((gate * jax.nn.sigmoid(gate) * up).astype(BF), weights_bf[1])
            squares = mapped * mapped
            high = squares.astype(BF)
            low = (squares - high.astype(F32)).astype(BF)
            ones = jnp.ones((8, 256), BF)
            row_src[b, i] = mm_nt(ones, high) + mm_nt(ones, low)
            if i == 0:
                map_dst[b, 0] = mapped.astype(BF)
            else:
                map_src[b, i - 1] = mapped.astype(BF)

    def send_rows(b):
        for dy, dz, r, t, row in ROUTES:
            remote(
                row_src.at[b, row // 256, :, pl.ds(row % 256, HALF)], row_dst.at[b, r - 1, :, pl.ds(t, HALF)],
                row_s.at[b], row_r.at[b], chip(-dy, -dz),
            ).start()

    def rows_all(b):
        return remote(row_dst.at[b], row_dst.at[b], row_s.at[b], row_r.at[b], twin)

    def send_back(b):
        for dy, dz, r, t, row in ROUTES:
            remote(
                map_src.at[b, row // 256 - 1, pl.ds(row % 256, HALF)], map_dst.at[b, r, pl.ds(t, HALF)],
                back_s.at[b], back_r.at[b], chip(-dy, -dz),
            ).start()

    def back_all(b):
        return remote(map_src.at[b], map_src.at[b], back_s.at[b], back_r.at[b], twin)

    def send_squares(b):
        sq_src[b] = row_src[b, 0] + row_dst[b, 0] + row_dst[b, 1] + row_dst[b, 2]
        for s in range(1, size_x):
            remote(sq_src.at[b], sq_dst.at[b, s - 1], sq_s.at[b], sq_r.at[b], across(s)).start()

    def squares_all(b):
        return remote(sq_dst.at[b], sq_dst.at[b], sq_s.at[b], sq_r.at[b], twin)

    def store(b):
        return pltpu.make_async_copy(raw_out.at[b], out_hbm.at[b], store_sem.at[b])

    def finish(b):
        total = sq_src[b]
        for s in range(1, size_x):
            total = total + sq_dst[b, s - 1]
        scale = lax.rsqrt(total * (1.0 / (total_heads * 256)) + 1e-06)
        scale = jnp.transpose(jnp.broadcast_to(scale[0:1, :], (128, 256)))
        gains = [gain_ref[pl.ds((r + own) & 3, 1), :] for r in range(4)]
        for g in range(4):
            for r in range(4):
                for c in range(2):
                    for k in range(2):
                        t = 64 * g + 32 * k
                        cols = slice(128 * c, 128 * c + 128)
                        tile = map_dst[b, r, t : t + 32, cols].astype(F32) * scale[t : t + 32, :]
                        tile = tile * gains[r][:, cols]
                        tile_buf[g, 64 * r + 32 * c : 64 * r + 32 * c + 32, 128 * k : 128 * k + 128] = tile.astype(BF)
            out = mm(scatter, tile_buf[g]).astype(BF)
            raw_out[b, 512 * g : 512 * g + 256, :] = out[:, :128]
            raw_out[b, 512 * g + 256 : 512 * g + 512, :] = out[:, 128:]
        store(b).start()

    sent = []

    def send(start, whole, b):
        start(b)
        sent.append(whole(b))

    def got(copy):
        copy.wait_recv()

    def forward(b):
        send_forward(b)
        sent.append(forward_all(b))

    def later_queries():
        send(send_query, query_all, 0)
        send(send_query, query_all, 1)

    def serve(b):
        apply(b, (3, 1, 2))
        send(send_rows, rows_all, b)
        send(send_back, back_all, b)
        apply(b, (0,))

    steps = [
        lambda: split_heads(KEY, 0),
        lambda: split_heads(TGT, 0),
        lambda: pl.semaphore_wait(barrier, len(greeted)),
        lambda: send(send_moved, moved_all, 0),
        lambda: send_own(0),
        load_weights,
        lambda: split_heads(KEY, 1),
        lambda: split_heads(TGT, 1),
        lambda: split_heads(QRY, 0),
        lambda: split_heads(QRY, 1),
        lambda: send_own(1),
        lambda: forward(0),
        lambda: gradients(0, 0),
        lambda: got(forward_all(0)),
        lambda: gradients(0, 1),
        lambda: send(send_ring, ring_all, 0),
        lambda: send(send_moved, moved_all, 1),
        lambda: got(ring_all(0)),
        lambda: send(send_all, all_all, 0),
        later_queries,
        lambda: forward(1),
        lambda: got(all_all(0)),
        lambda: send(send_twin, twin_copy, 0),
        lambda: got(twin_copy(0)),
        lambda: update(0),
        lambda: got(forward_all(1)),
        lambda: gradients(1, 0),
        lambda: gradients(1, 1),
        lambda: send(send_ring, ring_all, 1),
        lambda: got(query_all(0)),
        lambda: serve(0),
        lambda: got(ring_all(1)),
        lambda: send(send_all, all_all, 1),
        lambda: got(rows_all(0)),
        lambda: send(send_squares, squares_all, 0),
        lambda: got(squares_all(0)),
        lambda: got(back_all(0)),
        lambda: finish(0),
        lambda: got(all_all(1)),
        lambda: send(send_twin, twin_copy, 1),
        lambda: got(twin_copy(1)),
        lambda: update(1),
        lambda: got(query_all(1)),
        lambda: serve(1),
        lambda: got(rows_all(1)),
        lambda: send(send_squares, squares_all, 1),
        lambda: got(back_all(1)),
        lambda: got(squares_all(1)),
        lambda: finish(1),
        lambda: store(0).wait(),
        lambda: store(1).wait(),
    ]
    for step in steps:
        step()
    for copy in sent:
        copy.wait_send()


def per_device(size_z, size_x, queries, key_input, value_input, token_rates, fast_weights, update_rate, out_gain):
    piece = 384 // size_z

    def flat(a):
        return a.reshape(2, 256, 4, 2, 128).transpose(0, 1, 3, 2, 4).reshape(2, 2048, 128)

    hbm = pl.BlockSpec(memory_space=pltpu.HBM)
    dma = pltpu.SemaphoreType.DMA
    out = pl.pallas_call(
        functools.partial(kernel, size_z, size_x),
        out_shape=jax.ShapeDtypeStruct((2, 2048, 128), BF),
        in_specs=[hbm] * 7,
        out_specs=hbm,
        scratch_shapes=[
            pltpu.VMEM((3, 2, 2048, 128), BF),
            pltpu.VMEM((2, 4, 256), F32),
            pltpu.SMEM((4, 3), F32),
            pltpu.VMEM((4, 256), F32),
            pltpu.VMEM((2, 2048, 128), BF),
            pltpu.VMEM((2, 2, 2, 1024, 256), BF),
            pltpu.VMEM((2, 2, 3, 256, 256), BF),
            pltpu.VMEM((2, 1024, 256), BF),
            pltpu.VMEM((2, 3, 256, 256), BF),
            pltpu.VMEM((3, 256, 256), F32),
            pltpu.VMEM((3, 256, 256), BF),
            pltpu.VMEM((256, 256), BF),
            pltpu.VMEM((128, 256), BF),
            pltpu.VMEM((2, 1024, 128), BF),
            pltpu.VMEM((2, 1024, 256), BF),
            pltpu.VMEM((size_z, piece, 256), F32),
            pltpu.VMEM((2, size_z, piece, 256), BF),
            pltpu.VMEM((2, size_z - 1, piece, 256), BF),
            pltpu.VMEM((2, 2, size_z, piece, 256), BF),
            pltpu.VMEM((2, 3, 256, 256), BF),
            pltpu.VMEM((2, 4, 256, 256), BF),
            pltpu.VMEM((4, 256, 256), BF),
            pltpu.VMEM((2, 4, 8, 256), F32),
            pltpu.VMEM((2, 3, 8, 256), F32),
            pltpu.VMEM((2, 8, 256), F32),
            pltpu.VMEM((2, max(size_x - 1, 1), 8, 256), F32),
            dma((3, 2)), dma, dma((3,)), dma((2,)),
            dma((2,)), dma((2, len(ROUTES))),
            *[dma((2,)) for _ in range(16)],
        ],
        compiler_params=pltpu.CompilerParams(
            collective_id=0, has_side_effects=True, vmem_limit_bytes=60 * 1024 * 1024
        ),
        cost_estimate=pl.CostEstimate(flops=12_000_000_000, bytes_accessed=5_000_000, transcendentals=1_000_000),
    )(flat(queries), flat(key_input), flat(value_input), token_rates, fast_weights, update_rate, out_gain)
    return out.reshape(2, 256, 2, 4, 128).transpose(0, 1, 3, 2, 4).reshape(2, 256, 4, 256)


def solution(mesh):
    size_z = mesh.shape["tok"] // (2 * SIZE_Y)
    return jax.shard_map(
        functools.partial(per_device, size_z, mesh.shape["head"]),
        mesh=mesh,
        in_specs=(
            P(None, "tok", "head", None),
            P(None, "tok", "head", None),
            P(None, "tok", "head", None),
            P(None, "head", "tok"),
            P("head", None, None, None),
            P("head", None),
            P("head", None),
        ),
        out_specs=P(None, "tok", "head", None),
        check_vma=False,
    )
```

time: 84.4 us -> 73.6 us (0.87)
  Pallas kernels: 77.4 us -> 70.9 us
  local copies, waits for them, and re-layouts: 6.71 us -> 2.56 us
    pallas_call x1, Pallas kernels: 77.4 us -> 70.9 us  [per_device(): pl.pallas_call(functools.partial(kernel, size_z, size_x), out_shape=jax.S...]
    unnamed x13 -> x1, local copies, waits for them, and re-layouts: 6.71 us -> 2.56 us
where the time goes in v2:
time: 73.6 us; the launch traced here: 73.5 us
  Pallas kernels  70.9 us (96%)
  local copies, waits for them, and re-layouts  2.56 us (3%)
    pallas_call x1, Pallas kernels, per_device(): pl.pallas_call(functools.partial(kernel, size_z, size_x), out_shape=jax.S...  70.9 us
    unnamed x1, local copies, waits for them, and re-layouts  2.56 us

profile of v2, /device:TPU:1, one launch (start us, length us, event | category | flops | bytes accessed | tf_op | source)
XLA Modules:
  0.0 73.5 jit_solution(3392502640637558142)
XLA Ops:
  0.0 70.9 %shard_map.73 = bf16[2,2048,128]{2,1,0:T(8,128)(2,1)} custom-call(bf16[2,2048,128]{2,1,0:T(8,128)(2,1)} %bitcast.21, bf16[2,2048,128]{2,1,0:T(8,128)(2,1)} %bitcast.22, bf16[2,2048,128]{2,1,0:T(8,128)(2,1)} %bitcast.23, f32[2,4,256]{2,1,0:T(4,128)} %rate_hbm.1, f32[4,3,256,256]{3,2,1,0:T(8,128)} %w_hbm.1, f32[4,3]{1,0:T(4,128)} %lr_hbm.1, f32[4,256]{1,0:T(4,128)} %gain_hbm.1), custom_call_target="tpu_custom_call" | custom-call | flops 12000000000 | bytes 5000000 | tf_op jit(solution)/shard_map/pallas_call | solution.py:442
  70.9 2.6 %copy.13 = bf16[2,256,4,256]{3,2,1,0:T(4,128)(2,1)} copy(bf16[2,256,4,256]{3,2,1,0:T(4,128)(2,1)} %bitcast.20) | data formatting | bytes 2097152

commit v3 on v2

--- a/solution.py
+++ b/solution.py
@@ -28,6 +28,14 @@
     (0, -1, 3, 0, 512),
     (1, 0, 3, 128, 640),
 )
+MOVES = (
+    (-1, 1, 2, 0, 128, 768),
+    (1, -1, 2, 128, 128, 896),
+    (0, 1, 1, 0, 128, 256),
+    (-1, 0, 1, 128, 128, 384),
+    (0, -1, 3, 0, 128, 512),
+    (1, 0, 3, 128, 128, 640),
+)
 
 
 def mm(a, b):
@@ -44,11 +52,11 @@
 
 def kernel(
     size_z, size_x,
-    q_hbm, k_hbm, v_hbm, rate_hbm, w_hbm, lr_hbm, gain_hbm, out_hbm,
-    raw, rate_ref, lr_ref, gain_ref, raw_out, moved, staged, query, query_staged,
+    q_hbm, k_hbm, v_hbm, w_hbm, small_ref, out_ref,
+    raw, laid, moved, staged, query, query_staged,
     weights, weights_bf, w_gu, w_down, hid, cots, sums, ring_src, ring_dst, full,
     map_src, map_dst, tile_buf, row_src, row_dst, sq_src, sq_dst,
-    load_sem, w_sem, small_sem, store_sem, move_s, move_r, fwd_s, fwd_r, query_s, query_r,
+    near_sem, far_sem, load_sem, w_sem, move_s, move_r, fwd_s, fwd_r, query_s, query_r,
     ring_s, ring_r, all_s, all_r, twin_s, twin_r, row_s, row_r, back_s, back_r, sq_s, sq_r,
 ):
     bits_z = size_z.bit_length() - 1
@@ -77,8 +85,8 @@
         return pltpu.make_async_copy(sources[kind].at[b], raw.at[kind, b], load_sem.at[kind, b])
 
     barrier = pltpu.get_barrier_semaphore()
-    greeted = [chip(k, k) for k in peers]
-    greeted += [chip(dy, dz) for dy, dz, *_ in ROUTES]
+    near = [chip(dy, dz) for dy, dz, *_ in ROUTES]
+    greeted = [*near]
     greeted += [across(s) for s in range(1, size_x)]
     greeted += [chip(0, 0, 1)]
     load(KEY, 0).start()
@@ -86,14 +94,18 @@
     for device in greeted:
         pl.semaphore_signal(barrier, inc=1, device_id=device, device_id_type=MESH)
     w_load = pltpu.make_async_copy(w_hbm.at[own], weights, w_sem)
-    small = [
-        pltpu.make_async_copy(src, dst, small_sem.at[i])
-        for i, (src, dst) in enumerate([(rate_hbm, rate_ref), (lr_hbm, lr_ref), (gain_hbm, gain_ref)])
-    ]
-    for copy in [small[0], w_load, small[1], small[2]]:
-        copy.start()
+    w_load.start()
     for kind, b in ((KEY, 1), (TGT, 1), (QRY, 0), (QRY, 1)):
         load(kind, b).start()
+
+    def signal_near():
+        for device in near:
+            pl.semaphore_signal(near_sem, inc=1, device_id=device, device_id_type=MESH)
+
+    def signal_far():
+        pl.semaphore_wait(near_sem, len(near))
+        for dz in (2, -2):
+            pl.semaphore_signal(far_sem, inc=1, device_id=chip(0, dz), device_id_type=MESH)
 
     rows_i = lax.broadcasted_iota(jnp.int32, (256, 256), 0)
     cols_i = lax.broadcasted_iota(jnp.int32, (256, 256), 1)
@@ -107,11 +119,9 @@
     def split_heads(kind, b):
         load(kind, b).wait()
         if kind == TGT:
-            if b == 0:
-                small[0].wait()
             rates = []
             for r in range(4):
-                row = rate_ref[b, pl.ds((r + own) & 3, 1), :]
+                row = small_ref[b, pl.ds((r + own) & 3, 1), :]
                 rates.append(-jnp.transpose(jnp.broadcast_to(row, (128, 256))))
         for g in range(4):
             lo = raw[kind, b, 512 * g : 512 * g + 256, :]
@@ -143,34 +153,38 @@
     twin = chip(0, 0, 1)
 
     def moved_piece(b, i):
-        dy, dz, r, t, row = ROUTES[i]
+        dy, dz, r, t, n, row = MOVES[i]
         return remote(
-            staged.at[b, :, r - 1, pl.ds(t, HALF)],
-            moved.at[b, 0, :, pl.ds(row, HALF)],
+            staged.at[b, :, r - 1, pl.ds(t, n)],
+            moved.at[b, 0, :, pl.ds(row, n)],
             move_s.at[b], move_r.at[b, i], chip(dy, dz),
         )
 
     def send_moved(b):
-        for i in range(len(ROUTES)):
+        for i in range(len(MOVES)):
             moved_piece(b, i).start()
 
     def moved_all(b):
         return remote(staged.at[b], staged.at[b], move_s.at[b], move_r.at[b, 0], twin)
 
-    def forward_rows(b, row, n):
+    def forward_rows(b, at, row, n):
         rows = pl.ds(row, n)
-        return remote(moved.at[b, 0, :, rows], moved.at[b, 1, :, rows], fwd_s.at[b], fwd_r.at[b], twin)
+        return remote(moved.at[b, 0, :, rows], moved.at[b, 1, :, rows], fwd_s.at[b], fwd_r.at[b, at], twin)
 
     def send_own(b):
-        forward_rows(b, 0, 256).start()
-
-    def send_forward(b):
-        for i in (2, 3, 4, 5, 0, 1):
-            moved_piece(b, i).wait_recv()
-            forward_rows(b, ROUTES[i][-1], HALF).start()
+        forward_rows(b, 0, 0, 256).start()
+
+    def pass_on(b, at):
+        for i, (*_, n, row) in enumerate(MOVES):
+            if row // 256 == at:
+                moved_piece(b, i).wait_recv()
+                forward_rows(b, at, row, n).start()
+
+    def passed(b, at):
+        forward_rows(b, at, 256 * at, 256).wait_recv()
 
     def forward_all(b):
-        return remote(moved.at[b, 0], moved.at[b, 1], fwd_s.at[b], fwd_r.at[b], twin)
+        return remote(moved.at[b, 0], moved.at[b, 1], fwd_s.at[b], fwd_r.at[b, 0], twin)
 
     def send_query(b):
         for dy, dz, r, t, row in ROUTES:
@@ -182,8 +196,9 @@
     def query_all(b):
         return remote(query_staged.at[b], query_staged.at[b], query_s.at[b], query_r.at[b], twin)
 
-    def gradients(b, s):
-        for i in range(4):
+    def gradients(b, s, chunks=range(4), opens=False, closes=False):
+        all_rows = slice(256 * chunks[0], 256 * chunks[-1] + 256)
+        for i in chunks:
             rows = slice(256 * i, 256 * i + 256)
             pre = mm(moved[b, s, KEY, rows, :], w_gu[...])
             gate_pre, up_pre = pre[:, :HALF], pre[:, HALF:]
@@ -193,16 +208,14 @@
             hid[s, rows, :] = (act * up_pre).astype(BF)
             cots[s, rows, :HALF] = (back * up_pre * sg * (1.0 + gate_pre * (1.0 - sg))).astype(BF)
             cots[s, rows, HALF:] = (back * act).astype(BF)
-        grad_gu = mm_tn(moved[b, s, KEY], cots[s]).reshape(size_z, rows_gu, 256)
-        grad_down = mm_tn(hid[s], moved[b, s, TGT]).reshape(size_z, rows_down, 256)
-        if s == 0:
-            sums[:, :rows_gu, :] = grad_gu
-            sums[:, rows_gu:, :] = grad_down
-        else:
+        grad_gu = mm_tn(moved[b, s, KEY, all_rows, :], cots[s, all_rows, :]).reshape(size_z, rows_gu, 256)
+        grad_down = mm_tn(hid[s, all_rows, :], moved[b, s, TGT, all_rows, :]).reshape(size_z, rows_down, 256)
+        if not opens:
             grad_gu = sums[:, :rows_gu, :] + grad_gu
             grad_down = sums[:, rows_gu:, :] + grad_down
-            sums[:, :rows_gu, :] = grad_gu
-            sums[:, rows_gu:, :] = grad_down
+        sums[:, :rows_gu, :] = grad_gu
+        sums[:, rows_gu:, :] = grad_down
+        if closes:
             ring_src[b, :, :rows_gu, :] = grad_gu.astype(BF)
             ring_src[b, :, rows_gu:, :] = grad_down.astype(BF)
 
@@ -245,8 +258,6 @@
 
     def load_weights():
         w_load.wait()
-        small[1].wait()
-        small[2].wait()
         for m in range(3):
             set_weights(m, weights[m])
 
@@ -277,7 +288,7 @@
                     x = x * inverse[m]
                 xs[m] = x.astype(BF)
         for m in range(3):
-            new = weights[m] - lr_ref[own, m] * xs[m].astype(F32)
+            new = weights[m] - small_ref[3, pl.ds(own, 1), :][:, m : m + 1] * xs[m].astype(F32)
             weights[m] = new
             set_weights(m, new)
 
@@ -325,8 +336,18 @@
     def squares_all(b):
         return remote(sq_dst.at[b], sq_dst.at[b], sq_s.at[b], sq_r.at[b], twin)
 
-    def store(b):
-        return pltpu.make_async_copy(raw_out.at[b], out_hbm.at[b], store_sem.at[b])
+    def lay_out(b):
+        for g in range(4):
+            for r in range(4):
+                for c in range(2):
+                    for k in range(2):
+                        t = 64 * g + 32 * k
+                        tile_buf[g, 64 * r + 32 * c : 64 * r + 32 * c + 32, 128 * k : 128 * k + 128] = map_dst[
+                            b, r, t : t + 32, 128 * c : 128 * c + 128
+                        ]
+            out = mm(scatter, tile_buf[g]).astype(BF)
+            laid[b, 512 * g : 512 * g + 256, :] = out[:, :128]
+            laid[b, 512 * g + 256 : 512 * g + 512, :] = out[:, 128:]
 
     def finish(b):
         total = sq_src[b]
@@ -334,20 +355,9 @@
             total = total + sq_dst[b, s - 1]
         scale = lax.rsqrt(total * (1.0 / (total_heads * 256)) + 1e-06)
         scale = jnp.transpose(jnp.broadcast_to(scale[0:1, :], (128, 256)))
-        gains = [gain_ref[pl.ds((r + own) & 3, 1), :] for r in range(4)]
-        for g in range(4):
-            for r in range(4):
-                for c in range(2):
-                    for k in range(2):
-                        t = 64 * g + 32 * k
-                        cols = slice(128 * c, 128 * c + 128)
-                        tile = map_dst[b, r, t : t + 32, cols].astype(F32) * scale[t : t + 32, :]
-                        tile = tile * gains[r][:, cols]
-                        tile_buf[g, 64 * r + 32 * c : 64 * r + 32 * c + 32, 128 * k : 128 * k + 128] = tile.astype(BF)
-            out = mm(scatter, tile_buf[g]).astype(BF)
-            raw_out[b, 512 * g : 512 * g + 256, :] = out[:, :128]
-            raw_out[b, 512 * g + 256 : 512 * g + 512, :] = out[:, 128:]
-        store(b).start()
+        gain = jnp.concatenate([small_ref[2, :, :128], small_ref[2, :, 128:]], axis=0)
+        out = laid[b].astype(F32).reshape(256, 8, 128) * scale[:, None, :] * gain[None, :, :]
+        out_ref[b] = out.reshape(2048, 128).astype(BF)
 
     sent = []
 
@@ -358,9 +368,19 @@
     def got(copy):
         copy.wait_recv()
 
-    def forward(b):
-        send_forward(b)
-        sent.append(forward_all(b))
+    def first_gradients():
+        sent.append(forward_all(0))
+        for at in (1, 2, 3):
+            pass_on(0, at)
+        gradients(0, 0, opens=True)
+        for at in range(4):
+            passed(0, at)
+        gradients(0, 1, closes=True)
+
+    def later_tokens():
+        for at in (1, 2, 3):
+            pass_on(1, at)
+        sent.append(forward_all(1))
 
     def later_queries():
         send(send_query, query_all, 0)
@@ -378,29 +398,29 @@
         lambda: pl.semaphore_wait(barrier, len(greeted)),
         lambda: send(send_moved, moved_all, 0),
         lambda: send_own(0),
+        signal_near,
         load_weights,
         lambda: split_heads(KEY, 1),
         lambda: split_heads(TGT, 1),
+        signal_far,
         lambda: split_heads(QRY, 0),
         lambda: split_heads(QRY, 1),
         lambda: send_own(1),
-        lambda: forward(0),
-        lambda: gradients(0, 0),
-        lambda: got(forward_all(0)),
-        lambda: gradients(0, 1),
+        first_gradients,
+        lambda: pl.semaphore_wait(far_sem, 2),
         lambda: send(send_ring, ring_all, 0),
         lambda: send(send_moved, moved_all, 1),
         lambda: got(ring_all(0)),
         lambda: send(send_all, all_all, 0),
         later_queries,
-        lambda: forward(1),
+        later_tokens,
         lambda: got(all_all(0)),
         lambda: send(send_twin, twin_copy, 0),
         lambda: got(twin_copy(0)),
         lambda: update(0),
-        lambda: got(forward_all(1)),
-        lambda: gradients(1, 0),
-        lambda: gradients(1, 1),
+        lambda: [passed(1, at) for at in range(4)],
+        lambda: gradients(1, 0, opens=True),
+        lambda: gradients(1, 1, closes=True),
         lambda: send(send_ring, ring_all, 1),
         lambda: got(query_all(0)),
         lambda: serve(0),
@@ -408,8 +428,9 @@
         lambda: send(send_all, all_all, 1),
         lambda: got(rows_all(0)),
         lambda: send(send_squares, squares_all, 0),
+        lambda: got(back_all(0)),
+        lambda: lay_out(0),
         lambda: got(squares_all(0)),
-        lambda: got(back_all(0)),
         lambda: finish(0),
         lambda: got(all_all(1)),
         lambda: send(send_twin, twin_copy, 1),
@@ -420,10 +441,9 @@
         lambda: got(rows_all(1)),
         lambda: send(send_squares, squares_all, 1),
         lambda: got(back_all(1)),
+        lambda: lay_out(1),
         lambda: got(squares_all(1)),
         lambda: finish(1),
-        lambda: store(0).wait(),
-        lambda: store(1).wait(),
     ]
     for step in steps:
         step()
@@ -437,18 +457,18 @@
     def flat(a):
         return a.reshape(2, 256, 4, 2, 128).transpose(0, 1, 3, 2, 4).reshape(2, 2048, 128)
 
+    small = jnp.concatenate(
+        [token_rates, out_gain[None], jnp.pad(update_rate, ((0, 0), (0, 253)))[None]], axis=0
+    )
     hbm = pl.BlockSpec(memory_space=pltpu.HBM)
     dma = pltpu.SemaphoreType.DMA
     out = pl.pallas_call(
         functools.partial(kernel, size_z, size_x),
         out_shape=jax.ShapeDtypeStruct((2, 2048, 128), BF),
-        in_specs=[hbm] * 7,
-        out_specs=hbm,
+        in_specs=[hbm] * 4 + [pl.BlockSpec(memory_space=pltpu.VMEM)],
+        out_specs=pl.BlockSpec(memory_space=pltpu.VMEM),
         scratch_shapes=[
             pltpu.VMEM((3, 2, 2048, 128), BF),
-            pltpu.VMEM((2, 4, 256), F32),
-            pltpu.SMEM((4, 3), F32),
-            pltpu.VMEM((4, 256), F32),
             pltpu.VMEM((2, 2048, 128), BF),
             pltpu.VMEM((2, 2, 2, 1024, 256), BF),
             pltpu.VMEM((2, 2, 3, 256, 256), BF),
@@ -471,15 +491,16 @@
             pltpu.VMEM((2, 3, 8, 256), F32),
             pltpu.VMEM((2, 8, 256), F32),
             pltpu.VMEM((2, max(size_x - 1, 1), 8, 256), F32),
-            dma((3, 2)), dma, dma((3,)), dma((2,)),
-            dma((2,)), dma((2, len(ROUTES))),
-            *[dma((2,)) for _ in range(16)],
+            pltpu.SemaphoreType.REGULAR, pltpu.SemaphoreType.REGULAR,
+            dma((3, 2)), dma,
+            dma((2,)), dma((2, len(MOVES))), dma((2,)), dma((2, 4)),
+            *[dma((2,)) for _ in range(14)],
         ],
         compiler_params=pltpu.CompilerParams(
-            collective_id=0, has_side_effects=True, vmem_limit_bytes=60 * 1024 * 1024
+            collective_id=0, has_side_effects=True, vmem_limit_bytes=53760 * 1024
         ),
         cost_estimate=pl.CostEstimate(flops=12_000_000_000, bytes_accessed=5_000_000, transcendentals=1_000_000),
-    )(flat(queries), flat(key_input), flat(value_input), token_rates, fast_weights, update_rate, out_gain)
+    )(flat(queries), flat(key_input), flat(value_input), fast_weights, small)
     return out.reshape(2, 256, 2, 4, 128).transpose(0, 1, 3, 2, 4).reshape(2, 256, 4, 256)
 
 

time: 73.6 us -> 70.5 us (0.958)
  Pallas kernels: 70.9 us -> 68 us
  local copies, waits for them, and re-layouts: 2.56 us -> 1.66 us
    pallas_call x1, Pallas kernels: 70.9 us -> 68 us  [per_device(): pl.pallas_call(functools.partial(kernel, size_z, size_x), out_shape=jax.S...]
    unnamed x1, local copies, waits for them, and re-layouts: 2.56 us -> 0.97 us
where the time goes in v3:
time: 70.5 us; the launch traced here: 70.3 us
  Pallas kernels  68 us (96%)
  local copies, waits for them, and re-layouts  1.66 us (2%)
  other arithmetic  0.72 us (1%)
    pallas_call x1, Pallas kernels, per_device(): pl.pallas_call(functools.partial(kernel, size_z, size_x), out_shape=jax.S...  68 us

profile of v3, /device:TPU:1, one launch (start us, length us, event | category | flops | bytes accessed | tf_op | source)
XLA Modules:
  0.0 70.3 jit_solution(17973500308855201228)
XLA Ops:
  0.0 0.7 pad_bitcast_fusion
  0.7 0.7 %pad_maximum_fusion.small_ref = f32[4,4,256]{2,1,0:T(4,128)S(1)} fusion(f32[1,4,256]{2,1,0:T(4,128)S(1)} %pad_bitcast_fusion, f32[1,4,256]{2,1,0:T(4,128)} %bitcast.24, f32[2,4,256]{2,1,0:T(4,128)} %param.10), kind=kLoop, calls=%fused_computation | loop fusion | flops 8192 | bytes 32768 | tf_op jit(solution)/shard_map/concatenate | solution.py:460
  1.4 68.0 %shard_map.73 = bf16[2,2048,128]{2,1,0:T(8,128)(2,1)S(1)} custom-call(bf16[2,2048,128]{2,1,0:T(8,128)(2,1)} %bitcast.25, bf16[2,2048,128]{2,1,0:T(8,128)(2,1)} %bitcast.26, bf16[2,2048,128]{2,1,0:T(8,128)(2,1)} %bitcast.27, f32[4,3,256,256]{3,2,1,0:T(8,128)} %w_hbm.1, f32[4,4,256]{2,1,0:T(4,128)S(1)} %pad_maximum_fusion.small_ref), custom_call_target="tpu_custom_call" | custom-call | flops 12000000000 | bytes 5000000 | tf_op jit(solution)/shard_map/pallas_call | solution.py:465
  69.4 1.0 %copy.13 = bf16[2,256,4,256]{3,2,1,0:T(4,128)(2,1)} copy(bf16[2,256,4,256]{3,2,1,0:T(4,128)(2,1)S(1)} %bitcast.23) | data formatting | bytes 2097152

commit v4 on v3

--- a/solution.py
+++ b/solution.py
@@ -160,9 +160,17 @@
             move_s.at[b], move_r.at[b, i], chip(dy, dz),
         )
 
+    def send_kind(kind, b):
+        for i, (dy, dz, r, t, n, row) in enumerate(MOVES):
+            remote(
+                staged.at[b, kind, r - 1, pl.ds(t, n)],
+                moved.at[b, 0, kind, pl.ds(row, n)],
+                move_s.at[b], move_r.at[b, i], chip(dy, dz),
+            ).start()
+
     def send_moved(b):
-        for i in range(len(MOVES)):
-            moved_piece(b, i).start()
+        send_kind(KEY, b)
+        send_kind(TGT, b)
 
     def moved_all(b):
         return remote(staged.at[b], staged.at[b], move_s.at[b], move_r.at[b, 0], twin)
@@ -235,16 +243,26 @@
             total = total + ring_dst[b, k - 1].astype(F32)
         full[b, core, z] = total.astype(BF)
         for k in peers:
-            remote(full.at[b, core, z], full.at[b, core, z], all_s.at[b], all_r.at[b], chip(k, k)).start()
+            all_piece(b, z, k).start()
+        twin_piece(b, z).start()
+
+    def all_piece(b, at, k):
+        return remote(full.at[b, core, at], full.at[b, core, at], all_s.at[b], all_r.at[b, k], chip(k, k))
 
     def all_all(b):
-        return remote(ring_dst.at[b], ring_dst.at[b], all_s.at[b], all_r.at[b], twin)
+        return remote(ring_dst.at[b], ring_dst.at[b], all_s.at[b], all_r.at[b, 0], twin)
+
+    def twin_piece(b, at):
+        return remote(full.at[b, core, at], full.at[b, core, at], twin_s.at[b], twin_r.at[b], twin)
 
     def twin_copy(b):
         return remote(full.at[b, core], full.at[b, core], twin_s.at[b], twin_r.at[b], twin)
 
     def send_twin(b):
-        twin_copy(b).start()
+        for k in reversed(peers):
+            at = (z - k) & (size_z - 1)
+            all_piece(b, at, k).wait_recv()
+            twin_piece(b, at).start()
 
     def set_weights(m, new):
         wide = new.astype(BF)
@@ -386,17 +404,16 @@
         send(send_query, query_all, 0)
         send(send_query, query_all, 1)
 
-    def serve(b):
-        apply(b, (3, 1, 2))
+    def send_mapped(b):
         send(send_rows, rows_all, b)
         send(send_back, back_all, b)
-        apply(b, (0,))
 
     steps = [
         lambda: split_heads(KEY, 0),
+        lambda: pl.semaphore_wait(barrier, len(greeted)),
+        lambda: send_kind(KEY, 0),
         lambda: split_heads(TGT, 0),
-        lambda: pl.semaphore_wait(barrier, len(greeted)),
-        lambda: send(send_moved, moved_all, 0),
+        lambda: send(lambda b: send_kind(TGT, b), moved_all, 0),
         lambda: send_own(0),
         signal_near,
         load_weights,
@@ -412,10 +429,10 @@
         lambda: send(send_moved, moved_all, 1),
         lambda: got(ring_all(0)),
         lambda: send(send_all, all_all, 0),
-        later_queries,
+        lambda: send(send_query, query_all, 0),
         later_tokens,
-        lambda: got(all_all(0)),
         lambda: send(send_twin, twin_copy, 0),
+        lambda: send(send_query, query_all, 1),
         lambda: got(twin_copy(0)),
         lambda: update(0),
         lambda: [passed(1, at) for at in range(4)],
@@ -423,23 +440,26 @@
         lambda: gradients(1, 1, closes=True),
         lambda: send(send_ring, ring_all, 1),
         lambda: got(query_all(0)),
-        lambda: serve(0),
+        lambda: apply(0, range(4)),
         lambda: got(ring_all(1)),
         lambda: send(send_all, all_all, 1),
+        lambda: send_twin(1),
+        lambda: sent.append(twin_copy(1)),
+        lambda: send_mapped(0),
+        lambda: got(twin_copy(1)),
+        lambda: update(1),
+        lambda: got(query_all(1)),
+        lambda: apply(1, (3, 1, 2)),
+        lambda: send_mapped(1),
+        lambda: apply(1, (0,)),
         lambda: got(rows_all(0)),
         lambda: send(send_squares, squares_all, 0),
         lambda: got(back_all(0)),
         lambda: lay_out(0),
+        lambda: got(rows_all(1)),
+        lambda: send(send_squares, squares_all, 1),
         lambda: got(squares_all(0)),
         lambda: finish(0),
-        lambda: got(all_all(1)),
-        lambda: send(send_twin, twin_copy, 1),
-        lambda: got(twin_copy(1)),
-        lambda: update(1),
-        lambda: got(query_all(1)),
-        lambda: serve(1),
-        lambda: got(rows_all(1)),
-        lambda: send(send_squares, squares_all, 1),
         lambda: got(back_all(1)),
         lambda: lay_out(1),
         lambda: got(squares_all(1)),
@@ -457,8 +477,10 @@
     def flat(a):
         return a.reshape(2, 256, 4, 2, 128).transpose(0, 1, 3, 2, 4).reshape(2, 2048, 128)
 
-    small = jnp.concatenate(
-        [token_rates, out_gain[None], jnp.pad(update_rate, ((0, 0), (0, 253)))[None]], axis=0
+    small = (
+        lax.pad(token_rates, 0.0, ((0, 2, 0), (0, 0, 0), (0, 0, 0)))
+        + lax.pad(out_gain[None], 0.0, ((2, 1, 0), (0, 0, 0), (0, 0, 0)))
+        + lax.pad(update_rate[None], 0.0, ((3, 0, 0), (0, 0, 0), (0, 253, 0)))
     )
     hbm = pl.BlockSpec(memory_space=pltpu.HBM)
     dma = pltpu.SemaphoreType.DMA
@@ -494,7 +516,7 @@
             pltpu.SemaphoreType.REGULAR, pltpu.SemaphoreType.REGULAR,
             dma((3, 2)), dma,
             dma((2,)), dma((2, len(MOVES))), dma((2,)), dma((2, 4)),
-            *[dma((2,)) for _ in range(14)],
+            *[dma((2,)) for _ in range(5)], dma((2, size_z)), *[dma((2,)) for _ in range(8)],
         ],
         compiler_params=pltpu.CompilerParams(
             collective_id=0, has_side_effects=True, vmem_limit_bytes=53760 * 1024

time: 70.5 us -> 69.8 us (0.990)
    add x0 -> x1, other arithmetic: none -> 0.73 us  [per_device(): lax.pad(token_rates, 0.0, ((0, 2, 0), (0, 0, 0), (0, 0, 0)))]
    concatenate x1 -> x0, other arithmetic: 0.72 us -> none  [per_device(): jnp.concatenate([token_rates, out_gain[None], jnp.pad(update_rate, ((0, 0...]
where the time goes in v4:
time: 69.8 us; the launch traced here: 69.6 us
  Pallas kernels  67.9 us (97%)
  local copies, waits for them, and re-layouts  0.97 us (1%)
  other arithmetic  0.73 us (1%)
    pallas_call x1, Pallas kernels, per_device(): pl.pallas_call(functools.partial(kernel, size_z, size_x), out_shape=jax.S...  67.9 us

profile of v4, /device:TPU:1, one launch (start us, length us, event | category | flops | bytes accessed | tf_op | source)
XLA Modules:
  0.0 69.6 jit_solution(5728257850028611685)
XLA Ops:
  0.0 0.7 %pad_add_fusion.small_ref = f32[4,4,256]{2,1,0:T(4,128)S(1)} fusion(f32[1,4,3]{2,1,0:T(4,128)} %bitcast.24, f32[1,4,256]{2,1,0:T(4,128)} %bitcast.23, f32[2,4,256]{2,1,0:T(4,128)} %param.10), kind=kLoop, calls=%fused_computation | loop fusion | flops 8192 | bytes 28720 | tf_op jit(solution)/shard_map/add | solution.py:481
  0.7 67.9 %shard_map.73 = bf16[2,2048,128]{2,1,0:T(8,128)(2,1)S(1)} custom-call(bf16[2,2048,128]{2,1,0:T(8,128)(2,1)} %bitcast.25, bf16[2,2048,128]{2,1,0:T(8,128)(2,1)} %bitcast.26, bf16[2,2048,128]{2,1,0:T(8,128)(2,1)} %bitcast.27, f32[4,3,256,256]{3,2,1,0:T(8,128)} %w_hbm.1, f32[4,4,256]{2,1,0:T(4,128)S(1)} %pad_add_fusion.small_ref), custom_call_target="tpu_custom_call" | custom-call | flops 12000000000 | bytes 5000000 | tf_op jit(solution)/shard_map/pallas_call | solution.py:487
  68.6 1.0 %copy.13 = bf16[2,256,4,256]{3,2,1,0:T(4,128)(2,1)} copy(bf16[2,256,4,256]{3,2,1,0:T(4,128)(2,1)S(1)} %bitcast.22) | data formatting | bytes 2097152

commit v5 on v4

--- a/solution.py
+++ b/solution.py
@@ -227,8 +227,11 @@
             ring_src[b, :, :rows_gu, :] = grad_gu.astype(BF)
             ring_src[b, :, rows_gu:, :] = grad_down.astype(BF)
 
+    def turned(k):
+        return k + core * (size_z - 2 * k)
+
     def send_ring(b):
-        for k in peers:
+        for k in map(turned, peers):
             remote(
                 ring_src.at[b, (z + k) & (size_z - 1)], ring_dst.at[b, k - 1],
                 ring_s.at[b], ring_r.at[b], chip(k, k),
@@ -242,7 +245,7 @@
         for k in peers:
             total = total + ring_dst[b, k - 1].astype(F32)
         full[b, core, z] = total.astype(BF)
-        for k in peers:
+        for k in map(turned, peers):
             all_piece(b, z, k).start()
         twin_piece(b, z).start()
 

time: 69.8 us -> 69.6 us (level)
  no operation moved by 1% of the time
where the time goes in v5:
time: 69.6 us; the launch traced here: 69.4 us
  Pallas kernels  67.7 us (97%)
  local copies, waits for them, and re-layouts  0.97 us (1%)
  other arithmetic  0.73 us (1%)
    pallas_call x1, Pallas kernels, per_device(): pl.pallas_call(functools.partial(kernel, size_z, size_x), out_shape=jax.S...  67.7 us

profile of v5, /device:TPU:1, one launch (start us, length us, event | category | flops | bytes accessed | tf_op | source)
XLA Modules:
  0.0 69.4 jit_solution(18293264073640990615)
XLA Ops:
  0.0 0.7 %pad_add_fusion.small_ref = f32[4,4,256]{2,1,0:T(4,128)S(1)} fusion(f32[1,4,3]{2,1,0:T(4,128)} %bitcast.24, f32[1,4,256]{2,1,0:T(4,128)} %bitcast.23, f32[2,4,256]{2,1,0:T(4,128)} %param.10), kind=kLoop, calls=%fused_computation | loop fusion | flops 8192 | bytes 28720 | tf_op jit(solution)/shard_map/add | solution.py:484
  0.7 67.7 %shard_map.73 = bf16[2,2048,128]{2,1,0:T(8,128)(2,1)S(1)} custom-call(bf16[2,2048,128]{2,1,0:T(8,128)(2,1)} %bitcast.25, bf16[2,2048,128]{2,1,0:T(8,128)(2,1)} %bitcast.26, bf16[2,2048,128]{2,1,0:T(8,128)(2,1)} %bitcast.27, f32[4,3,256,256]{3,2,1,0:T(8,128)} %w_hbm.1, f32[4,4,256]{2,1,0:T(4,128)S(1)} %pad_add_fusion.small_ref), custom_call_target="tpu_custom_call" | custom-call | flops 12000000000 | bytes 5000000 | tf_op jit(solution)/shard_map/pallas_call | solution.py:490
  68.5 1.0 %copy.13 = bf16[2,256,4,256]{3,2,1,0:T(4,128)(2,1)} copy(bf16[2,256,4,256]{3,2,1,0:T(4,128)(2,1)S(1)} %bitcast.22) | data formatting | bytes 2097152
